TPU v7x, 128 devices: a whole 4x4x4 slice. The times are simulated.
128 devices in a mesh: pipe: 2 (over y_hi), seq: 16 (over x, z), dp: 4 (over y_lo, core).
Axes of the slice: x: 4, y: 4 (y_hi: 2, y_lo: 2; y = y_hi * 2 + y_lo), z: 4, core: 2. Of those that a mesh axis runs over, the one named last changes fastest.
Arguments:
- queries: bfloat16 [2, 4, 16, 384, 1536], P('pipe', 'dp', 'seq'), may hold values from -18 to 18
- keys: bfloat16 [2, 4, 16, 384, 1536], P('pipe', 'dp', 'seq'), may hold values from -18 to 18
- values: bfloat16 [2, 4, 16, 384, 1536], P('pipe', 'dp', 'seq'), may hold values from -6 to 6
- grad_out: bfloat16 [2, 4, 16, 384, 1536], P('pipe', 'dp', 'seq'), may hold values from -20 to 20
- norm_gains: float32 [2, 2, 128], P('pipe'), may hold values from 0.5 to 1.5
- kv_tiles: int32 [2, 4, 16, 3], P('pipe', 'dp', 'seq'), may hold values from -1 to 15, as said below
Outputs:
- qkv_grad: bfloat16 [2, 3, 4, 16, 384, 1536], P('pipe', None, 'dp', 'seq')
- gain_grads: float32 [2, 2, 128], P('pipe')
Inputs may be any that keep to these rules, and one draw needn't show every extreme that they name: `kv_tiles`: tile t covers frame tile t // 1 and spatial tile t % 1. The row of tile t names tile t itself and some of the other tiles of frame tiles t - 1, t // 1 and t + 1 inside the sample, each at most once, in some order; its other entries are -1.
All inputs are finite; a program needn't handle non-finite values.
Results may differ from a plain program's by a relative error of at most 0.007.
Values may be sent and summed in bfloat16 or wider, within the bound.
A program may use at most 256 MiB of HBM per device.

v0:
```python
import math
import jax
import jax.numpy as jnp
from jax import lax
from jax.sharding import PartitionSpec as P

HEADS = 12
HEAD_DIM = 128
epsilon = 1e-06


def padded(shard, sides, width):
    for axis, dim in sides:
        size, length = (lax.axis_size(axis), shard.shape[dim])
        up = [(i, (i + 1) % size) for i in range(size - 1)]
        down = [(j, i) for i, j in up]
        last = lax.slice_in_dim(shard, length - width, length, axis=dim)
        initial = lax.slice_in_dim(shard, 0, width, axis=dim)
        before = lax.ppermute(last, axis, up)
        after = lax.ppermute(initial, axis, down)
        shard = jnp.concatenate([before, shard, after], axis=dim)
    return shard


def passed_along(value, axis, steps):
    count = lax.axis_size(axis)
    initial, last = (max(0, -steps), min(count, count - steps))
    return lax.ppermute(value, axis, [(source, source + steps) for source in range(initial, last)])


def passed_along_2(value, axis, steps):
    count = lax.axis_size(axis)
    pairs = [(source, (source + steps) % count) for source in range(count)]
    return lax.ppermute(value, axis, pairs)


def normalize(source, gain_row):
    floats = source.astype(jnp.float32).reshape(source.shape[:-1] + (HEADS, HEAD_DIM))
    scaled = lax.rsqrt(jnp.mean(floats * floats, axis=-1, keepdims=True) + epsilon)
    normed = (floats * scaled * gain_row).astype(jnp.bfloat16).reshape(source.shape)
    return (normed, floats, scaled)


def norm_back(grad_hat, floats, scaled, gain_row):
    projected = jnp.sum(gain_row * grad_hat * floats, axis=-1, keepdims=True)
    gradient = scaled * gain_row * grad_hat - scaled**3 * floats * projected / HEAD_DIM
    gain_part = jnp.sum((grad_hat * floats * scaled).reshape(-1, HEAD_DIM), axis=0)
    return (gradient.reshape(gradient.shape[:-2] + (HEADS * HEAD_DIM,)), gain_part)


def score_block(query_head, grad_head, key_head, value_head, key_mask):
    root_scale = HEAD_DIM ** (-0.5)
    scores = (
        jnp.einsum("nqhd,nkhd->nhqk", query_head, key_head, preferred_element_type=jnp.float32)
        * root_scale
    )
    exp_scores = jnp.exp(scores) * key_mask[:, None, None, :]
    grad_attn = jnp.einsum(
        "nqhd,nkhd->nhqk", grad_head, value_head, preferred_element_type=jnp.float32
    )
    totals = jnp.sum(exp_scores, axis=-1, keepdims=True)
    attention = exp_scores / totals
    deltas = jnp.sum(attention * grad_attn, axis=-1, keepdims=True)
    dscore = (attention * (grad_attn - deltas)).astype(jnp.bfloat16)
    return (dscore, attention.astype(jnp.bfloat16), totals, deltas)


def spread(slot_grad, targets, list_slots, target_span):
    row_count, key_rows, head_count, head_width = slot_grad.shape
    shaped = slot_grad.reshape(
        row_count * list_slots, key_rows // list_slots, head_count * head_width
    )
    flat_targets = targets.reshape(-1)
    placed = jnp.where(flat_targets >= 0, flat_targets, target_span)
    totals = jnp.zeros(
        (target_span + 1, key_rows // list_slots, head_count * head_width), jnp.float32
    )
    return totals.at[placed].add(shaped)[:target_span]


def tile_pass(
    query_hat, grad_in, key_gathered, value_gathered, key_mask, targets, list_slots, target_span
):
    row_count, tile_rows, lane_total = query_hat.shape
    key_rows = key_gathered.shape[1]
    root_scale = HEAD_DIM ** (-0.5)
    query_parts, key_parts, value_parts, total_parts, delta_parts = ([], [], [], [], [])
    for first_head in range(0, HEADS, 2):
        lane_span = slice(first_head * HEAD_DIM, (first_head + 2) * HEAD_DIM)
        query_head = query_hat[:, :, lane_span].reshape(row_count, tile_rows, 2, HEAD_DIM)
        grad_head = grad_in[:, :, lane_span].reshape(row_count, tile_rows, 2, HEAD_DIM)
        key_head = key_gathered[:, :, lane_span].reshape(row_count, key_rows, 2, HEAD_DIM)
        value_head = value_gathered[:, :, lane_span].reshape(row_count, key_rows, 2, HEAD_DIM)
        dscore, attn_low, totals, deltas = score_block(
            query_head, grad_head, key_head, value_head, key_mask
        )
        query_parts.append(
            jnp.einsum("nhqk,nkhd->nqhd", dscore, key_head, preferred_element_type=jnp.float32)
            * root_scale
        )
        key_slot = (
            jnp.einsum("nhqk,nqhd->nkhd", dscore, query_head, preferred_element_type=jnp.float32)
            * root_scale
        )
        value_slot = jnp.einsum(
            "nhqk,nqhd->nkhd", attn_low, grad_head, preferred_element_type=jnp.float32
        )
        key_parts.append(spread(key_slot, targets, list_slots, target_span))
        value_parts.append(spread(value_slot, targets, list_slots, target_span))
        total_parts.append(totals[..., 0])
        delta_parts.append(deltas[..., 0])
    query_grads = jnp.concatenate(query_parts, axis=2)
    return (
        query_grads,
        jnp.concatenate(key_parts, axis=-1),
        jnp.concatenate(value_parts, axis=-1),
        jnp.concatenate(total_parts, axis=1),
        jnp.concatenate(delta_parts, axis=1),
    )


def local(queries, keys, values, grad_out, norm_gains, kv_tiles):
    query_in = queries[0, 0]
    key_in = keys[0, 0]
    value_in = values[0, 0]
    grad_in = grad_out[0, 0]
    gain_rows = norm_gains[0]
    tile_lists = kv_tiles[0, 0]
    tiles_here, tile_rows, lane_total = query_in.shape
    list_slots = tile_lists.shape[1]
    position = lax.axis_index("seq")
    seq_count = lax.axis_size("seq")
    query_hat, query_floats, query_scale = normalize(query_in, gain_rows[0])
    key_hat, key_floats, key_scale = normalize(key_in, gain_rows[1])
    rim_pairs = padded(jnp.stack([key_hat, value_in]), (("seq", 1),), tiles_here)
    live_slots = tile_lists >= 0
    key_mask = jnp.repeat(live_slots.astype(jnp.float32), tile_rows, axis=1)
    local_ids = tile_lists - (position - 1) * tiles_here
    fetch_ids = jnp.clip(local_ids, 0, 3 * tiles_here - 1)
    key_gathered = rim_pairs[0][fetch_ids].reshape(tiles_here, list_slots * tile_rows, lane_total)
    value_gathered = rim_pairs[1][fetch_ids].reshape(tiles_here, list_slots * tile_rows, lane_total)
    targets = jnp.where(live_slots, local_ids, -1)
    target_span = 3 * tiles_here
    query_hat_grad, key_acc, value_acc, totals, deltas = tile_pass(
        query_hat, grad_in, key_gathered, value_gathered, key_mask, targets, list_slots, target_span
    )
    query_grad, query_gain = norm_back(query_hat_grad, query_floats, query_scale, gain_rows[0])
    query_low = query_grad.astype(jnp.bfloat16)
    from_right = passed_along(jnp.stack([key_acc[:tiles_here], value_acc[:tiles_here]]), "seq", -1)
    from_left = passed_along(
        jnp.stack([key_acc[2 * tiles_here :], value_acc[2 * tiles_here :]]), "seq", 1
    )
    key_hat_grad = key_acc[tiles_here : 2 * tiles_here] + from_right[0] + from_left[0]
    value_grad = value_acc[tiles_here : 2 * tiles_here] + from_right[1] + from_left[1]
    key_grad, key_gain = norm_back(
        key_hat_grad.reshape(tiles_here, tile_rows, HEADS, HEAD_DIM),
        key_floats,
        key_scale,
        gain_rows[1],
    )
    summed = lax.psum(jnp.stack([query_gain, key_gain]), ("seq", "dp"))
    gain_grads = summed / math.sqrt(
        lax.axis_size("dp") * seq_count * tiles_here * tile_rows * HEADS
    )
    key_low = key_grad.astype(jnp.bfloat16)
    value_low = value_grad.astype(jnp.bfloat16)
    passed = passed_along_2(jnp.stack([query_low, key_low, value_low]), "pipe", -1)
    return (passed[None, :, None], gain_grads[None])


def solution(mesh):
    placed = (
        P("pipe", "dp", "seq", None, None),
        P("pipe", "dp", "seq", None, None),
        P("pipe", "dp", "seq", None, None),
        P("pipe", "dp", "seq", None, None),
        P("pipe", None, None),
        P("pipe", "dp", "seq", None),
    )
    return jax.shard_map(
        local,
        mesh=mesh,
        in_specs=placed,
        out_specs=(P("pipe", None, "dp", "seq", None, None), P("pipe", None, None)),
        check_vma=False,
    )
```

profile of v0, /device:TPU:16, one launch (start us, length us, event | category | flops | bytes accessed | tf_op | source)
XLA Modules:
  0.0 747.3 jit_solution(4585193369530839053)
XLA Ops:
  10.4 5.3 collective-permute-start
  40.4 24.8 %collective-permute-done = bf16[2,1,384,1536]{3,2,1,0:T(8,128)(2,1)} collective-permute-done((bf16[2,1,384,1536]{3,2,1,0:T(8,128)(2,1)}, bf16[2,1,384,1536]{3,2,1,0:T(8,128)(2,1)}, u32[]{:S(2)}, u32[]{:S(2)}) %collective-permute-start) | collective-permute-done | bytes 2359328 | tf_op jit(solution)/shard_map/ppermute | solution.py:19
  65.2 5.5 collective-permute-done.1
  70.7 3.9 pad_maximum_fusion
  74.6 3.8 slice_bitcast_fusion
  78.4 4.7 gather_fusion.1
  87.6 4.7 gather_fusion
  92.3 3.6 fusion.84
  98.0 3.6 convolution_bitcast_fusion.5
  101.6 5.2 multiply_reduce_fusion.5
  106.8 4.0 convolution_bitcast_fusion.11
  110.8 3.6 multiply_convert_fusion.5
  122.2 5.2 multiply_reduce_fusion.4
  127.5 4.0 convolution_bitcast_fusion.10
  131.5 3.7 multiply_convert_fusion.4
  139.4 3.6 convolution_bitcast_fusion.3
  143.0 5.2 multiply_reduce_fusion.3
  148.2 4.0 convolution_bitcast_fusion.9
  152.2 3.8 multiply_convert_fusion.3
  160.3 3.6 convolution_bitcast_fusion.2
  163.8 5.2 multiply_reduce_fusion.2
  169.1 4.0 convolution_bitcast_fusion.8
  173.0 3.7 multiply_convert_fusion.2
  181.0 3.6 convolution_bitcast_fusion.1
  184.6 5.2 multiply_reduce_fusion.1
  189.8 4.0 convolution_bitcast_fusion.7
  193.8 3.7 multiply_convert_fusion.1
  198.8 3.8 convolution_bitcast_fusion
  202.6 5.0 multiply_reduce_fusion
  207.7 4.0 convolution_bitcast_fusion.6
  211.6 3.7 multiply_convert_fusion
  291.0 3.6 scatter_fusion.5
  297.0 5.0 slice_bitcast_fusion.9
  302.0 4.3 copy.292
  308.3 4.7 copy.289
  322.5 4.3 copy.295
  328.8 4.9 copy.298
  335.7 4.7 copy.301
  342.4 4.7 copy.304
  394.5 6.7 collective-permute-start.3
  420.8 74.6 %collective-permute-done.2 = f32[2,1,384,1536]{3,2,1,0:T(8,128)} collective-permute-done((f32[2,1,384,1536]{3,2,1,0:T(8,128)}, f32[2,1,384,1536]{3,2,1,0:T(8,128)}, u32[]{:S(2)}, u32[]{:S(2)}) %collective-permute-start.2) | collective-permute-done | bytes 4718624 | tf_op jit(solution)/shard_map/ppermute | solution.py:28
  495.4 3.7 collective-permute-done.3
  499.0 7.3 fusion.21
  508.3 4.9 multiply_reduce_fusion.8
  522.7 4.5 fusion.65
  549.2 3.6 multiply_reduce_fusion.6
  552.9 189.6 %psum.7 = f32[2,128]{1,0:T(2,128)S(1)} all-reduce(f32[2,128]{1,0:T(2,128)S(1)} %pad_maximum_fusion.5), channel_id=1, replica_groups=mesh['pipe'=2,'seq'=16,'dp'=4] {'seq','dp'}, use_global_device_ids=true, to_apply=%region_31.32 | all-reduce | flops 256 | bytes 2048 | tf_op jit(solution)/shard_map/psum | solution.py:161
  743.0 4.0 copy.394
  (289 shorter events, 259.1 us)
Async XLA Ops:
  7.0 15.9 %copy-start.70 = (f32[128]{0:T(128)}, f32[128]{0:T(128)S(1)}, u32[]{:S(2)}) copy-start(f32[128]{0:T(128)S(1)} %get-tuple-element.45) | copy-start | bytes 1540
  8.8 8.3 %copy-start.55 = (bf16[1,1,1,384,1536]{4,3,2,1,0:T(8,128)(2,1)S(1)}, bf16[1,1,1,384,1536]{4,3,2,1,0:T(8,128)(2,1)}, u32[]{:S(2)}) copy-start(bf16[1,1,1,384,1536]{4,3,2,1,0:T(8,128)(2,1)} %param.9) | copy-start | bytes 3538948
  10.4 8.1 %copy-start.7 = (bf16[1,1,1,384,1536]{4,3,2,1,0:T(8,128)(2,1)S(1)}, bf16[1,1,1,384,1536]{4,3,2,1,0:T(8,128)(2,1)}, u32[]{:S(2)}) copy-start(bf16[1,1,1,384,1536]{4,3,2,1,0:T(8,128)(2,1)} %param.6) | copy-start | bytes 3538948
  10.4 54.8 %collective-permute-start = (bf16[2,1,384,1536]{3,2,1,0:T(8,128)(2,1)}, bf16[2,1,384,1536]{3,2,1,0:T(8,128)(2,1)}, u32[]{:S(2)}, u32[]{:S(2)}) collective-permute-start(bf16[2,1,384,1536]{3,2,1,0:T(8,128)(2,1)} %pad_maximum_fusion.4), channel_id=1, source_target_pairs={{0,4},{4,8},{8,12},{12,16},{16,20},{20,24},{24,28},{28,32},{32,36}... | collective-permute-start | bytes 7077896 | tf_op jit(solution)/shard_map/ppermute | solution.py:19
  15.8 54.9 %collective-permute-start.1 = (bf16[2,1,384,1536]{3,2,1,0:T(8,128)(2,1)}, bf16[2,1,384,1536]{3,2,1,0:T(8,128)(2,1)}, u32[]{:S(2)}, u32[]{:S(2)}) collective-permute-start(bf16[2,1,384,1536]{3,2,1,0:T(8,128)(2,1)} %pad_maximum_fusion.4), channel_id=1, source_target_pairs={{4,0},{8,4},{12,8},{16,12},{20,16},{24,20},{28,24},{32,28},{36,32}... | collective-permute-start | bytes 7077896 | tf_op jit(solution)/shard_map/ppermute | solution.py:20
  20.7 380.5 %copy-start = (f32[384,12,128]{0,2,1:T(8,128)}, f32[384,12,128]{0,2,1:T(8,128)S(1)}, u32[]{:S(2)}) copy-start(f32[384,12,128]{0,2,1:T(8,128)S(1)} %mul.607) | copy-start | bytes 7077892
  26.0 44.7 %copy-start.24 = (bf16[1,1,384,1536]{3,2,1,0:T(8,128)(2,1)S(1)}, bf16[1,1,384,1536]{3,2,1,0:T(8,128)(2,1)}, u32[]{:S(2)}) copy-start(bf16[1,1,384,1536]{3,2,1,0:T(8,128)(2,1)} %copy-done.23) | copy-start | bytes 3538948
  36.6 34.1 %copy-start.33 = (bf16[1,1,1,384,1536]{4,3,2,1,0:T(8,128)(2,1)S(1)}, bf16[1,1,1,384,1536]{4,3,2,1,0:T(8,128)(2,1)}, u32[]{:S(2)}) copy-start(bf16[1,1,1,384,1536]{4,3,2,1,0:T(8,128)(2,1)} %param.8) | copy-start | bytes 3538948
  106.8 4.0 copy-start.18
  127.5 4.0 copy-start.19
  148.2 4.0 copy-start.20
  169.1 4.0 copy-start.21
  189.8 4.0 copy-start.22
  198.8 8.9 %copy-start.52 = (bf16[1,1152,256]{1,2,0:T(8,128)(2,1)}, bf16[1,1152,256]{1,2,0:T(8,128)(2,1)S(1)}, u32[]{:S(2)}) copy-start(bf16[1,1152,256]{1,2,0:T(8,128)(2,1)S(1)} %copy.364) | copy-start | bytes 1769476
  198.8 3.8 copy-start.56
  202.6 5.0 copy-start.54
  207.7 4.0 copy-start.17
  211.6 3.7 copy-start.10
  211.6 3.7 copy-start.58
  258.2 4.5 copy-start.36
  265.9 3.9 copy-start.42
  273.1 3.8 copy-start.40
  280.1 3.8 copy-start.39
  287.2 3.8 copy-start.38
  297.0 5.0 copy-start.34
  354.1 3.8 copy-start.45
  361.2 3.9 copy-start.44
  368.3 3.8 copy-start.43
  375.3 3.9 copy-start.37
  385.1 3.1 copy-start.30
  388.2 3.9 copy-start.29
  390.8 104.6 %collective-permute-start.2 = (f32[2,1,384,1536]{3,2,1,0:T(8,128)}, f32[2,1,384,1536]{3,2,1,0:T(8,128)}, u32[]{:S(2)}, u32[]{:S(2)}) collective-permute-start(f32[2,1,384,1536]{3,2,1,0:T(8,128)} %pad_maximum_fusion.1), channel_id=1, source_target_pairs={{4,0},{8,4},{12,8},{16,12},{20,16},{24,20},{28,24},{32,28},{36,32}... | collective-permute-start | bytes 14155784 | tf_op jit(solution)/shard_map/ppermute | solution.py:28
  394.5 104.5 %collective-permute-start.3 = (f32[2,1,384,1536]{3,2,1,0:T(8,128)}, f32[2,1,384,1536]{3,2,1,0:T(8,128)}, u32[]{:S(2)}, u32[]{:S(2)}) collective-permute-start(f32[2,1,384,1536]{3,2,1,0:T(8,128)} %pad_maximum_fusion.2), channel_id=1, source_target_pairs={{0,4},{4,8},{8,12},{12,16},{16,20},{20,24},{24,28},{28,32},{32,36}... | collective-permute-start | bytes 14155784 | tf_op jit(solution)/shard_map/ppermute | solution.py:28
  404.8 3.3 copy-start.4
  410.2 4.3 copy-start.48
  412.2 3.0 copy-start.13
  412.2 3.0 copy-start.49
  519.4 3.2 copy-start.6
  519.4 3.2 copy-start.65
  522.6 4.6 copy-start.8
  522.6 4.6 copy-start.25
  522.6 4.8 copy-start.26
  522.6 5.5 copy-start.27
  522.6 6.2 copy-start.28
  522.7 6.2 copy-start.67
  532.1 210.9 %collective-permute-start.4 = (bf16[3,1,384,1536]{3,2,1,0:T(8,128)(2,1)}, bf16[3,1,384,1536]{3,2,1,0:T(8,128)(2,1)}, u32[]{:S(2)}, u32[]{:S(2)}) collective-permute-start(bf16[3,1,384,1536]{3,2,1,0:T(8,128)(2,1)} %pad_maximum_fusion.3), channel_id=1, source_target_pairs={{0,64},{64,0},{1,65},{65,1},{2,66},{66,2},{3,67},{67,3},{4,68},{68... | collective-permute-start | bytes 10616840 | tf_op jit(solution)/shard_map/ppermute | solution.py:34
  537.7 3.1 copy-start.59
  541.6 3.2 copy-start.9
  (31 other events, 58.5 us)
where the time goes:
time: 754 us; the launch traced here: 747 us
  local copies, waits for them, and re-layouts  235 us (31%)
  blocking collectives  190 us (25%)
  waiting for transfers between devices  109 us (14%)
  other arithmetic  105 us (14%)
  matrix products  91.6 us (12%)
  starting transfers between devices  16.1 us (2%)
    psum x1, blocking collectives, local(): summed = lax.psum(jnp.stack([query_gain, key_gain]), ('seq', 'dp'))  190 us
    ppermute x2, waiting for transfers between devices, passed_along(): lax.ppermute(value, axis, [(source, source + steps) for source in range(i...  78.3 us
    unnamed x172, local copies, waits for them, and re-layouts  58.3 us
    scatter-add x12, other arithmetic, spread(): return totals.at[placed].add(shaped)[:target_span]  39.6 us
    div x6, matrix products, score_block(): attention = exp_scores / totals  31.2 us
    reshape x12, local copies, waits for them, and re-layouts, spread(): slot_grad.reshape(row_count * list_slots, key_rows // list_slots, head_co...  29.8 us
    transpose x6, local copies, waits for them, and re-layouts, tile_pass(): jnp.einsum('nhqk,nqhd->nkhd', attn_low, grad_head, preferred_element_type...  27.7 us
    ppermute x1, waiting for transfers between devices, padded(): before = lax.ppermute(last, axis, up)  24.8 us
  transfers between devices with their start and end apart: 5, of which 4 were waited for; matrix products, arithmetic and copies ran while one was open for 9% of the time, Pallas kernels for 0%

commit v1 on v0

--- a/solution.py
+++ b/solution.py
@@ -158,7 +158,7 @@
         key_scale,
         gain_rows[1],
     )
-    summed = lax.psum(jnp.stack([query_gain, key_gain]), ("seq", "dp"))
+    summed = lax.psum(lax.psum(jnp.stack([query_gain, key_gain]), "seq"), "dp")
     gain_grads = summed / math.sqrt(
         lax.axis_size("dp") * seq_count * tiles_here * tile_rows * HEADS
     )

time: 754 us -> 632 us (0.84)
  the two profiles are of different devices: /device:TPU:16 before, /device:TPU:6 now
where the time goes in v1:
time: 632 us; the launch traced here: 625 us
  local copies, waits for them, and re-layouts  235 us (37%)
  waiting for transfers between devices  112 us (18%)
  other arithmetic  106 us (17%)
  matrix products  91.6 us (14%)
  blocking collectives  58.1 us (9%)
  starting transfers between devices  20.1 us (3%)
    ppermute x2, waiting for transfers between devices, passed_along(): lax.ppermute(value, axis, [(source, source + steps) for source in range(i...  84.9 us
    unnamed x172, local copies, waits for them, and re-layouts  58.2 us
    psum x2, blocking collectives, local(): summed = lax.psum(lax.psum(jnp.stack([query_gain, key_gain]), 'seq'), 'dp')  58.1 us
    scatter-add x12, other arithmetic, spread(): return totals.at[placed].add(shaped)[:target_span]  40.8 us
    div x6, matrix products, score_block(): attention = exp_scores / totals  31.3 us
    reshape x12, local copies, waits for them, and re-layouts, spread(): slot_grad.reshape(row_count * list_slots, key_rows // list_slots, head_co...  29.8 us
    transpose x6, local copies, waits for them, and re-layouts, tile_pass(): jnp.einsum('nhqk,nqhd->nkhd', attn_low, grad_head, preferred_element_type...  27.7 us
    ppermute x1, waiting for transfers between devices, padded(): before = lax.ppermute(last, axis, up)  26.2 us
  transfers between devices with their start and end apart: 5, of which 4 were waited for; matrix products, arithmetic and copies ran while one was open for 10% of the time, Pallas kernels for 0%

profile of v1, /device:TPU:6, one launch (start us, length us, event | category | flops | bytes accessed | tf_op | source)
XLA Modules:
  0.0 625.1 jit_solution(16319423213384066589)
XLA Ops:
  10.4 3.9 collective-permute-start
  14.4 4.3 collective-permute-start.1
  42.1 26.2 %collective-permute-done = bf16[2,1,384,1536]{3,2,1,0:T(8,128)(2,1)} collective-permute-done((bf16[2,1,384,1536]{3,2,1,0:T(8,128)(2,1)}, bf16[2,1,384,1536]{3,2,1,0:T(8,128)(2,1)}, u32[]{:S(2)}, u32[]{:S(2)}) %collective-permute-start) | collective-permute-done | bytes 2359328 | tf_op jit(solution)/shard_map/ppermute | solution.py:19
  69.5 3.9 pad_maximum_fusion
  73.4 3.8 slice_bitcast_fusion
  77.2 4.7 gather_fusion.1
  86.4 4.7 gather_fusion
  91.1 3.7 fusion.84
  100.4 5.2 multiply_reduce_fusion.5
  105.7 3.9 convolution_bitcast_fusion.11
  109.6 3.6 multiply_convert_fusion.5
  121.1 5.2 multiply_reduce_fusion.4
  126.3 4.0 convolution_bitcast_fusion.10
  130.3 3.7 multiply_convert_fusion.4
  141.8 5.2 multiply_reduce_fusion.3
  147.1 4.0 convolution_bitcast_fusion.9
  151.1 3.8 multiply_convert_fusion.3
  159.2 3.6 convolution_bitcast_fusion.2
  162.7 5.2 multiply_reduce_fusion.2
  168.0 4.0 convolution_bitcast_fusion.8
  171.9 3.7 multiply_convert_fusion.2
  179.9 3.6 convolution_bitcast_fusion.1
  183.5 5.2 multiply_reduce_fusion.1
  188.7 4.0 convolution_bitcast_fusion.7
  192.7 3.7 multiply_convert_fusion.1
  197.7 3.8 convolution_bitcast_fusion
  201.5 5.0 multiply_reduce_fusion
  206.6 4.0 convolution_bitcast_fusion.6
  210.5 3.7 multiply_convert_fusion
  290.2 3.7 scatter_fusion.5
  296.5 5.0 slice_bitcast_fusion.9
  301.4 4.3 copy.292
  307.7 4.7 copy.289
  322.1 4.3 copy.295
  328.4 4.9 copy.298
  335.2 4.7 copy.301
  342.0 4.7 copy.304
  379.2 3.6 scatter_fusion.11
  390.9 6.6 %collective-permute-start.2 = (f32[2,1,384,1536]{3,2,1,0:T(8,128)}, f32[2,1,384,1536]{3,2,1,0:T(8,128)}, u32[]{:S(2)}, u32[]{:S(2)}) collective-permute-start(f32[2,1,384,1536]{3,2,1,0:T(8,128)} %pad_maximum_fusion.1), channel_id=1, source_target_pairs={{4,0},{8,4},{12,8},{16,12},{20,16},{24,20},{28,24},{32,28},{36,32}... | collective-permute-start | bytes 14155784 | tf_op jit(solution)/shard_map/ppermute | solution.py:28
  421.6 76.2 %collective-permute-done.2 = f32[2,1,384,1536]{3,2,1,0:T(8,128)} collective-permute-done((f32[2,1,384,1536]{3,2,1,0:T(8,128)}, f32[2,1,384,1536]{3,2,1,0:T(8,128)}, u32[]{:S(2)}, u32[]{:S(2)}) %collective-permute-start.2) | collective-permute-done | bytes 4718624 | tf_op jit(solution)/shard_map/ppermute | solution.py:28
  497.8 8.7 %collective-permute-done.3 = f32[2,1,384,1536]{3,2,1,0:T(8,128)} collective-permute-done((f32[2,1,384,1536]{3,2,1,0:T(8,128)}, f32[2,1,384,1536]{3,2,1,0:T(8,128)}, u32[]{:S(2)}, u32[]{:S(2)}) %collective-permute-start.3) | collective-permute-done | bytes 4718624 | tf_op jit(solution)/shard_map/ppermute | solution.py:28
  506.5 7.3 %fusion.21 = (f32[1,384,1536]{2,1,0:T(8,128)S(1)}, bf16[1,1,384,1536]{3,2,1,0:T(8,128)(2,1)}) fusion(f32[2,1,384,1536]{3,2,1,0:T(8,128)} %collective-permute-done.3, f32[2,1,384,1536]{3,2,1,0:T(8,128)} %collective-permute-done.2, f32[3,384,1536]{2,1,0:T(8,128)} %slice_dynamic-update-slice_fusion.6, f32[3,384,1536]{2,1,0:T(8,128)} %slice_dynamic-update-slice_fusion), kind=kLoop, calls=%fused_computation.80 | loop fusion | flops 2949120 | bytes 17694720 | tf_op jit(solution)/shard_map/add | solution.py:153
  515.8 4.9 multiply_reduce_fusion.8
  530.1 4.5 fusion.65
  558.6 3.6 multiply_reduce_fusion.6
  562.2 30.6 %psum.14 = f32[2,128]{1,0:T(2,128)S(1)} all-reduce(f32[2,128]{1,0:T(2,128)S(1)} %pad_maximum_fusion.5), channel_id=1, replica_groups=mesh['pipe'=2,'seq'=16,'dp'=4] {'seq'}, use_global_device_ids=true, to_apply=%region_31.32 | all-reduce | flops 256 | bytes 2048 | tf_op jit(solution)/shard_map/psum | solution.py:161
  592.8 27.4 %psum.15 = f32[2,128]{1,0:T(2,128)S(1)} all-reduce(f32[2,128]{1,0:T(2,128)S(1)} %psum.14), channel_id=1, replica_groups=mesh['pipe'=2,'seq'=16,'dp'=4] {'dp'}, use_global_device_ids=true, to_apply=%region_32.33 | all-reduce | flops 256 | bytes 2048 | tf_op jit(solution)/shard_map/psum | solution.py:161
  620.8 4.0 copy.394
  (290 shorter events, 266.4 us)
Async XLA Ops:
  7.0 17.5 %copy-start.70 = (f32[128]{0:T(128)}, f32[128]{0:T(128)S(1)}, u32[]{:S(2)}) copy-start(f32[128]{0:T(128)S(1)} %get-tuple-element.45) | copy-start | bytes 1540
  8.8 9.9 %copy-start.55 = (bf16[1,1,1,384,1536]{4,3,2,1,0:T(8,128)(2,1)S(1)}, bf16[1,1,1,384,1536]{4,3,2,1,0:T(8,128)(2,1)}, u32[]{:S(2)}) copy-start(bf16[1,1,1,384,1536]{4,3,2,1,0:T(8,128)(2,1)} %param.9) | copy-start | bytes 3538948
  10.4 9.8 %copy-start.7 = (bf16[1,1,1,384,1536]{4,3,2,1,0:T(8,128)(2,1)S(1)}, bf16[1,1,1,384,1536]{4,3,2,1,0:T(8,128)(2,1)}, u32[]{:S(2)}) copy-start(bf16[1,1,1,384,1536]{4,3,2,1,0:T(8,128)(2,1)} %param.6) | copy-start | bytes 3538948
  10.4 57.9 %collective-permute-start = (bf16[2,1,384,1536]{3,2,1,0:T(8,128)(2,1)}, bf16[2,1,384,1536]{3,2,1,0:T(8,128)(2,1)}, u32[]{:S(2)}, u32[]{:S(2)}) collective-permute-start(bf16[2,1,384,1536]{3,2,1,0:T(8,128)(2,1)} %pad_maximum_fusion.4), channel_id=1, source_target_pairs={{0,4},{4,8},{8,12},{12,16},{16,20},{20,24},{24,28},{28,32},{32,36}... | collective-permute-start | bytes 7077896 | tf_op jit(solution)/shard_map/ppermute | solution.py:19
  14.4 55.1 %collective-permute-start.1 = (bf16[2,1,384,1536]{3,2,1,0:T(8,128)(2,1)}, bf16[2,1,384,1536]{3,2,1,0:T(8,128)(2,1)}, u32[]{:S(2)}, u32[]{:S(2)}) collective-permute-start(bf16[2,1,384,1536]{3,2,1,0:T(8,128)(2,1)} %pad_maximum_fusion.4), channel_id=1, source_target_pairs={{4,0},{8,4},{12,8},{16,12},{20,16},{24,20},{28,24},{32,28},{36,32}... | collective-permute-start | bytes 7077896 | tf_op jit(solution)/shard_map/ppermute | solution.py:20
  22.4 379.4 %copy-start = (f32[384,12,128]{0,2,1:T(8,128)}, f32[384,12,128]{0,2,1:T(8,128)S(1)}, u32[]{:S(2)}) copy-start(f32[384,12,128]{0,2,1:T(8,128)S(1)} %mul.607) | copy-start | bytes 7077892
  27.6 41.9 %copy-start.24 = (bf16[1,1,384,1536]{3,2,1,0:T(8,128)(2,1)S(1)}, bf16[1,1,384,1536]{3,2,1,0:T(8,128)(2,1)}, u32[]{:S(2)}) copy-start(bf16[1,1,384,1536]{3,2,1,0:T(8,128)(2,1)} %copy-done.23) | copy-start | bytes 3538948
  38.2 31.3 %copy-start.33 = (bf16[1,1,1,384,1536]{4,3,2,1,0:T(8,128)(2,1)S(1)}, bf16[1,1,1,384,1536]{4,3,2,1,0:T(8,128)(2,1)}, u32[]{:S(2)}) copy-start(bf16[1,1,1,384,1536]{4,3,2,1,0:T(8,128)(2,1)} %param.8) | copy-start | bytes 3538948
  105.7 3.9 copy-start.18
  126.3 4.0 copy-start.19
  147.1 4.0 copy-start.20
  168.0 4.0 copy-start.21
  188.7 4.0 copy-start.22
  197.7 8.9 %copy-start.52 = (bf16[1,1152,256]{1,2,0:T(8,128)(2,1)}, bf16[1,1152,256]{1,2,0:T(8,128)(2,1)S(1)}, u32[]{:S(2)}) copy-start(bf16[1,1152,256]{1,2,0:T(8,128)(2,1)S(1)} %copy.364) | copy-start | bytes 1769476
  197.7 3.8 copy-start.56
  201.5 5.0 copy-start.54
  206.6 4.0 copy-start.17
  210.5 3.7 copy-start.10
  210.5 3.7 copy-start.58
  257.2 4.5 copy-start.36
  265.0 3.8 copy-start.42
  272.2 3.8 copy-start.40
  279.3 3.8 copy-start.39
  286.5 3.8 copy-start.38
  296.5 5.0 copy-start.34
  353.8 3.8 copy-start.45
  361.0 3.8 copy-start.44
  368.2 3.8 copy-start.43
  375.4 3.8 copy-start.37
  385.2 3.1 copy-start.30
  388.3 9.1 %copy-start.29 = (f32[1,1,384,1536]{3,2,1,0:T(8,128)S(1)}, f32[1,1,384,1536]{3,2,1,0:T(8,128)}, u32[]{:S(2)}) copy-start(f32[1,1,384,1536]{3,2,1,0:T(8,128)} %get-tuple-element.11) | copy-start | bytes 7077892
  390.9 106.9 %collective-permute-start.2 = (f32[2,1,384,1536]{3,2,1,0:T(8,128)}, f32[2,1,384,1536]{3,2,1,0:T(8,128)}, u32[]{:S(2)}, u32[]{:S(2)}) collective-permute-start(f32[2,1,384,1536]{3,2,1,0:T(8,128)} %pad_maximum_fusion.1), channel_id=1, source_target_pairs={{4,0},{8,4},{12,8},{16,12},{20,16},{24,20},{28,24},{32,28},{36,32}... | collective-permute-start | bytes 14155784 | tf_op jit(solution)/shard_map/ppermute | solution.py:28
  399.9 106.6 %collective-permute-start.3 = (f32[2,1,384,1536]{3,2,1,0:T(8,128)}, f32[2,1,384,1536]{3,2,1,0:T(8,128)}, u32[]{:S(2)}, u32[]{:S(2)}) collective-permute-start(f32[2,1,384,1536]{3,2,1,0:T(8,128)} %pad_maximum_fusion.2), channel_id=1, source_target_pairs={{0,4},{4,8},{8,12},{12,16},{16,20},{20,24},{24,28},{28,32},{32,36}... | collective-permute-start | bytes 14155784 | tf_op jit(solution)/shard_map/ppermute | solution.py:28
  405.4 3.3 copy-start.4
  410.9 4.3 copy-start.48
  412.9 3.0 copy-start.13
  412.9 3.0 copy-start.49
  526.8 3.2 copy-start.6
  526.8 3.2 copy-start.65
  530.0 4.6 copy-start.8
  530.0 4.6 copy-start.25
  530.1 4.8 copy-start.26
  530.1 5.5 copy-start.27
  530.1 6.2 copy-start.28
  530.1 6.2 copy-start.67
  539.5 81.3 %collective-permute-start.4 = (bf16[3,1,384,1536]{3,2,1,0:T(8,128)(2,1)}, bf16[3,1,384,1536]{3,2,1,0:T(8,128)(2,1)}, u32[]{:S(2)}, u32[]{:S(2)}) collective-permute-start(bf16[3,1,384,1536]{3,2,1,0:T(8,128)(2,1)} %pad_maximum_fusion.3), channel_id=1, source_target_pairs={{0,64},{64,0},{1,65},{65,1},{2,66},{66,2},{3,67},{67,3},{4,68},{68... | collective-permute-start | bytes 10616840 | tf_op jit(solution)/shard_map/ppermute | solution.py:34
  547.1 3.2 copy-start.59
  551.0 3.2 copy-start.9
  (31 other events, 58.8 us)
